TPU v7x, 32 devices: a whole 2x2x4 slice. The times are simulated.
32 devices in a mesh: dp: 8 (over z, y), mp: 4 (over x, core).
Axes of the slice: x: 2, y: 2, z: 4, core: 2. Of those that a mesh axis runs over, the one named last changes fastest.
Arguments:
- patches: bfloat16 [384, 50176], P('mp', 'dp'), may hold values from -6 to 6
- keep_mask: int32 [256, 196], P('dp'), may hold values from 0 to 1, as said below
- ln1_gain: bfloat16 [384], P('mp'), may hold values from 0.25 to 1.75
- ln1_bias: bfloat16 [384], P('mp'), may hold values from -3 to 3
- w_qkv: bfloat16 [384, 1152], P('mp'), may hold values from -0.3125 to 0.3125
- q_bias: bfloat16 [384], P('mp'), may hold values from -3 to 3
- v_bias: bfloat16 [384], P('mp'), may hold values from -3 to 3
- mix_pre: float32 [8, 8], replicated, may hold values from -3 to 3
- mix_post: float32 [8, 8], replicated, may hold values from -3 to 3
- w_proj: bfloat16 [384, 384], P('mp'), may hold values from -1.5 to 1.5
- proj_bias: bfloat16 [384], P('mp'), may hold values from -3 to 3
- gamma1: bfloat16 [384], P('mp'), may hold values from 0.25 to 1.75
- ln2_gain: bfloat16 [384], P('mp'), may hold values from 0.25 to 1.75
- ln2_bias: bfloat16 [384], P('mp'), may hold values from -3 to 3
- w_fc1: bfloat16 [384, 1536], P('mp'), may hold values from -0.3125 to 0.3125
- fc1_bias: bfloat16 [1536], P('mp'), may hold values from -3 to 3
- w_fc2: bfloat16 [1536, 384], P('mp'), may hold values from -0.15625 to 0.15625
- fc2_bias: bfloat16 [384], P('mp'), may hold values from -3 to 3
- gamma2: bfloat16 [384], P('mp'), may hold values from 0.25 to 1.75
- cotangent: bfloat16 [384, 50176], P('mp', 'dp'), may hold values from -6 to 6
Outputs:
- output: bfloat16 [384, 50176], P('mp', 'dp')
- input_grad: bfloat16 [384, 50176], P('mp', 'dp')
- ln1_gain_grad: float32 [384], P('mp')
- ln1_bias_grad: float32 [384], P('mp')
- w_qkv_grad: float32 [384, 1152], P('mp')
- q_bias_grad: float32 [384], P('mp')
- v_bias_grad: float32 [384], P('mp')
- mix_pre_grad: float32 [8, 8], replicated
- mix_post_grad: float32 [8, 8], replicated
- w_proj_grad: float32 [384, 384], P('mp')
- proj_bias_grad: float32 [384], P('mp')
- gamma1_grad: float32 [384], P('mp')
- ln2_gain_grad: float32 [384], P('mp')
- ln2_bias_grad: float32 [384], P('mp')
- w_fc1_grad: float32 [384, 1536], P('mp')
- fc1_bias_grad: float32 [1536], P('mp')
- w_fc2_grad: float32 [1536, 384], P('mp')
- fc2_bias_grad: float32 [384], P('mp')
- gamma2_grad: float32 [384], P('mp')
Inputs may be any that keep to these rules, and one draw needn't show every extreme that they name: `keep_mask`: entry 0 of every image is 1; the share of kept patches differs from image to image.
All inputs are finite; a program needn't handle non-finite values.
Results may differ from a plain program's by a relative error of at most 0.019.
Values may be sent and summed in bfloat16 or wider, within the bound.
A program may use at most 128 MiB of HBM per device.

v0:
```python
import functools
import jax
import jax.numpy as jnp
from jax import lax
from jax.experimental import pallas as pl
from jax.experimental.pallas import tpu as pltpu
from jax.sharding import PartitionSpec as P

PATCHES = 196
HEADS = 8
EPSILON = 1e-06
MASKED = -1000000000.0
F32 = jnp.float32
BF16 = jnp.bfloat16
VMEM_BYTES = 63 * 2 ** 20
LANES = 256
KEYS = 208


def dot(a, b):
    return lax.dot_general(a, b, (((1,), (0,)), ((), ())), preferred_element_type=F32)


def dot_nt(a, b):
    return lax.dot_general(a, b, (((1,), (1,)), ((), ())), preferred_element_type=F32)


def dot_tn(a, b):
    return lax.dot_general(a, b, (((0,), (0,)), ((), ())), preferred_element_type=F32)


def twice(col):
    return jnp.concatenate([col, col], axis=1)


def fold(v):
    r = v[:, :128]
    for i in range(128, v.shape[1], 128):
        r = r + v[:, i:i + 128]
    return r


def lane_column(row):
    return jnp.transpose(jnp.broadcast_to(row, (128, row.shape[1])))


def gelu_parts(h):
    e = jnp.exp(-0.5 * h * h)
    cum = 0.5 * (1.0 + lax.erf(h * 0.7071067811865476))
    return cum, cum + h * (e * 0.3989422804014327)


MESH = pl.DeviceIdType.MESH
TILE = 128
VECS = ("g1", "b1", "qb", "vb", "pb", "s1", "g2", "b2", "fb2", "s2")


class Plan:
    def __init__(self, n_dp, n_mp, patches, keep_mask, w_fc2):
        self.n_dp = n_dp
        self.n_mp = n_mp
        self.nx = n_mp // 2
        self.CS, self.cols = patches
        self.C = self.CS * n_mp
        self.FFS = w_fc2[0]
        self.FF = self.FFS * n_mp
        self.n_img = keep_mask[0] // n_mp
        self.tok = self.n_img * PATCHES
        starts = [self.tok * m for m in range(n_mp)]
        self.bases = [s // TILE * TILE for s in starts]
        self.shifts = [s % TILE for s in starts]
        top = max(self.shifts)
        self.width = -(-(self.tok + top) // TILE) * TILE
        self.wide = self.width + TILE
        self.pairs = self.n_img // 2
        self.in_cuts = [0] + [-(-(2 * PATCHES * (k + 1) + top) // TILE) * TILE for k in range(self.pairs)]
        self.out_cuts = [0] + [2 * PATCHES * (k + 1) // TILE * TILE for k in range(self.pairs - 1)] + [self.width]
        self.vrows = len(VECS) + self.FFS // self.CS
        self.off = {}
        at = 0
        for name in VECS + ("fb1",):
            w = self.FF if name == "fb1" else self.C
            self.off[name] = (at, w)
            at += w
        self.total = at
        self.long = (self.FFS // TILE, TILE) if self.FFS % TILE == 0 else (1, self.FFS)
        half = self.CS // 2
        self.groups = ((2, self.pieces(self.FFS // 2, n_dp // 2), True),
                       (2, self.pieces(half * (self.FF // self.C + 1), n_dp // 2), True))
        self.groups += ((1, self.pieces(self.CS, n_dp), False),) * 3
    def pieces(self, rows, cuts):
        return -(-rows // (16 * cuts)) * 16 * cuts

    def group_scratch(self, ny, half, lent):
        V = pltpu.VMEM
        nx, more, lanes, nz = self.nx, max(self.nx - 1, 1), self.C, self.n_dp // ny
        second = half if ny > 1 else 16
        return [V((16 if lent else nx * ny * half, lanes), BF16), V((nx, ny * half, lanes), BF16),
                V((nx, second, lanes), BF16), V((nx, second, lanes), BF16), V((more, half, lanes), BF16),
                V((more, half, lanes), BF16), V((half, lanes), BF16), V((nz, half // nz, lanes), BF16),
                V((half, lanes), BF16)]


class Group:
    def __init__(self, pn, ny, refs, blocks):
        self.pn, self.ny, self.blocks = pn, ny, blocks
        self.nz = pn.n_dp // ny
        self.s1, self.r1, self.s2, self.r2, self.s3, self.r3, self.s4, self.r4, self.s5, self.out = refs
        self.half = self.s4.shape[0]
        self.piece = self.half // self.nz

    def build(self, remote, local_copy, xi, core, sibling, dp):
        pn, half, ny = self.pn, self.half, self.ny
        self.xi, self.core = xi, core
        self.y, self.z = (dp % 2, dp // 2) if ny > 1 else (0, dp)
        other = dp + 1 - 2 * self.y
        used = pn.CS if ny == 1 else ny * half
        self.c1 = [remote(self.s1.at[pl.ds(ny * half * x, used), :], self.r1.at[x, pl.ds(0, used), :], {"mp": sibling})
                   for x in range(pn.nx)]
        self.c2 = []
        if ny > 1:
            self.c2 = [remote(self.s2.at[x], self.r2.at[x], {"dp": other}) for x in range(pn.nx)]
        used = pn.CS if ny == 1 else half
        self.c3 = [remote(self.s3.at[d - 1, pl.ds(0, used), :], self.r3.at[d - 1, pl.ds(0, used), :], {"mp": ((xi + d) % pn.nx) * 2 + core})
                   for d in range(1, pn.nx)]
        self.c4, self.c5 = [], []
        own = self.s5.at[self.rows(self.z)]
        for e in range(1, self.nz):
            to = (self.z + e) % self.nz
            self.c4.append(remote(self.s4.at[self.rows(to)], self.r4.at[e], {"dp": ny * to + self.y}))
            self.c5.append(remote(own, own, {"dp": ny * to + self.y}))
        there = self.out.at[pl.ds(pl.multiple_of(self.y * half, 16), half), :]
        self.c6 = [local_copy(self.s5, there)]
        if ny > 1:
            self.c6.append(remote(self.s5, there, {"dp": other}))

    def rows(self, q):
        return pl.ds(pl.multiple_of(q * self.piece, 16), self.piece)

    def fill(self, dst, j, y, add):
        lo = 0
        for v in self.blocks(j, y):
            at = slice(lo, lo + v.shape[0])
            dst[at, :] = add(at, v).astype(BF16)
            lo = at.stop

    def over_cores(self):
        half = self.half
        for x in range(self.pn.nx):
            for y in range(self.ny):
                self.fill(self.s1.at[pl.ds((self.ny * x + y) * half, half), :], 2 * x + 1 - self.core, y, lambda at, v: v)
            self.c1[x].start()

    def from_core(self, x, y, at):
        if self.ny == 1:
            return self.r1[x, at, :].astype(F32)
        upper = slice(at.start + self.half, at.stop + self.half)
        return jnp.where(y == 0, self.r1[x, at, :].astype(F32), self.r1[x, upper, :].astype(F32))

    def over_y(self):
        y = 1 - self.y
        for x in range(self.pn.nx):
            self.c1[x].wait_recv()
            self.fill(self.s2.at[x], 2 * x + self.core, y, lambda at, v: v + self.from_core(x, y, at))
            self.c2[x].start()

    def so_far(self, x, at, v):
        v = v + self.from_core(x, self.y, at)
        return v + self.r2[x, at, :].astype(F32) if self.ny > 1 else v

    def over_x(self):
        for c in self.c2 if self.ny > 1 else self.c1:
            c.wait_recv()
        for d in range(1, self.pn.nx):
            x = (self.xi + d) % self.pn.nx
            self.fill(self.s3.at[d - 1], 2 * x + self.core, self.y, lambda at, v: self.so_far(x, at, v))
            self.c3[d - 1].start()

    def over_z(self):
        for c in self.c3:
            c.wait_recv()

        def add(at, v):
            v = self.so_far(self.xi, at, v)
            for d in range(1, self.pn.nx):
                v = v + self.r3[d - 1, at, :].astype(F32)
            return v

        self.fill(self.s4, 2 * self.xi + self.core, self.y, add)
        for c in self.c4:
            c.start()

    def back_z(self):
        v = self.s4[self.rows(self.z), :].astype(F32)
        for e in range(1, self.nz):
            self.c4[e - 1].wait_recv()
            v = v + self.r4[e].astype(F32)
        self.s5[self.rows(self.z), :] = v.astype(BF16)
        for c in self.c5:
            c.start()

    def back_y(self):
        for c in self.c5:
            c.wait_recv()
        for c in self.c6:
            c.start()

    def finish(self):
        self.c6[0].wait()
        for c in self.c6[1:]:
            c.wait_recv()


def layer_kernel(pn, x_hbm, c_hbm, wqkv_hbm, wproj_hbm, wfc1_hbm, wfc2_hbm, keep_ref, pre_ref, post_ref, *rest):
    vec_refs, rest = rest[:len(VECS) + 1], rest[len(VECS) + 1:]
    layer_body(pn, x_hbm, c_hbm, wqkv_hbm, wproj_hbm, wfc1_hbm, wfc2_hbm, keep_ref, pre_ref, post_ref, vec_refs,
               *rest)


def layer_body(pn, x_hbm, c_hbm, wqkv_hbm, wproj_hbm, wfc1_hbm, wfc2_hbm, keep_ref, pre_ref, post_ref, vec_refs,
                 orecv_s, irecv_s, small_ref, r4_fc2, r4_fc1, r4_v, r4_k, r4_q,
                 xw_s, cw_s, pv_s, wqkv_s, wproj_s, wfc1_s, wfc2_s, wqkvT_s, wprojT_s, wfc1T_s, wfc2T_s,
                 x_s, first_s, qkv_s, p_s, a_s, gm_s, col_s, act_s, slope_s, gh_s, two_s, mrow_s, mask_s,
                 dqkv_ref, dproj_ref, dfc1_ref, dfc2_ref, dvec_ref, dmix_ref,
                 pack_s, hop1_s, pack2_s, hop2_s, pvec_ref, *rest):
    group_refs = [list(rest[9 * i:9 * i + 9]) + [r] for i, r in enumerate((r4_fc2, r4_fc1, r4_v, r4_k, r4_q))]
    group_refs[0][0], group_refs[1][0] = wfc1T_s, wfc2_s
    ssem, rsem, lsem = rest[45:]
    ow_s, iw_s = xw_s, cw_s
    C, CS, FF, n_img, n_mp, nx = pn.C, pn.CS, pn.FF, pn.n_img, pn.n_mp, pn.nx
    inv_c = 1.0 / C
    n_dp = pn.n_dp
    dp = lax.axis_index("dp")
    me = lax.axis_index("mp")
    core = me % 2
    xi = me // 2
    sibling = me + 1 - 2 * core
    my_shift = (pn.tok * me) % TILE

    count = [0, 0]
    sent = []

    def remote(src, dst, dev):
        i = count[0]
        count[0] += 1
        copy = pltpu.make_async_remote_copy(src_ref=src, dst_ref=dst, send_sem=ssem.at[i], recv_sem=rsem.at[i],
                                            device_id=dev, device_id_type=MESH)
        sent.append(copy)
        return copy

    def local_copy(src, dst):
        i = count[1]
        count[1] += 1
        return pltpu.make_async_copy(src, dst, lsem.at[i])

    def peer(d):
        return (me + d) % n_mp

    def aligned(v, n):
        return pl.multiple_of(v, n)

    def window(src, dst, k):
        lo, hi = pn.in_cuts[k], pn.in_cuts[k + 1]
        mine = dst.at[pl.ds(aligned(me * CS, CS), CS), pl.ds(lo, hi - lo)]

        def part(m):
            base = (pn.tok * m) // TILE * TILE
            return src.at[:, pl.ds(aligned(base + lo, TILE), hi - lo)]

        return [local_copy(part(me), mine)] + [remote(part(peer(d)), mine, {"mp": peer(d)}) for d in range(1, n_mp)]

    x_parts = [window(x_hbm, xw_s, k) for k in range(pn.pairs)]
    c_parts = [window(c_hbm, cw_s, k) for k in range(pn.pairs)]
    vec_parts = [local_copy(pvec_ref, pv_s.at[me])]
    vec_parts += [remote(pvec_ref, pv_s.at[me], {"mp": peer(d)}) for d in range(1, n_mp)]

    def weight(src, dst):
        rows = src.shape[0]

        def shard(m):
            return dst.at[pl.ds(aligned(m * rows, rows), rows), :]

        own = local_copy(src, shard(me))
        across = [remote(src, shard(me), {"mp": ((xi + d) % nx) * 2 + core}) for d in range(1, nx)]
        beside = remote(src, shard(me), {"mp": sibling})
        relay = []
        for d in range(1, nx):
            s = shard(((xi + nx - d) % nx) * 2 + core)
            relay.append(remote(s, s, {"mp": sibling}))
        return own, across, beside, relay

    def spread_weight(src, dst, block):
        rows = src.shape[0]

        def shard(m):
            return dst.at[pl.ds(aligned(m * rows, rows), rows), :]

        own = local_copy(src, shard(me))
        beside = remote(src, shard(me), {"mp": sibling})
        across = [remote(block(src, 0, quarter), block(dst, me * rows, quarter), {"mp": ((xi + d) % nx) * 2 + core})
                  for d in range(1, nx)]
        along, relay = [], []
        for d in range(1, nx):
            m = ((xi + nx - d) % nx) * 2 + core
            mine = block(dst, m * rows, quarter)
            along += [remote(mine, mine, {"dp": dp - quarter + (quarter + e) % 4}) for e in range(1, 4)]
            relay.append(remote(shard(m), shard(m), {"mp": sibling}))
        return own, across, beside, relay, along

    quarter = dp % 4

    def fc1_block(ref, row, q):
        return ref.at[pl.ds(aligned(row, 16), CS), pl.ds(aligned(q * (FF // 4), TILE), FF // 4)]

    def fc2_block(ref, row, q):
        rows = pn.FFS // 4
        return ref.at[pl.ds(aligned(row + q * rows, 16), rows), :]

    w_parts = [weight(s, d) for s, d in ((wqkv_hbm, wqkv_s), (wproj_hbm, wproj_s))]
    for s, d, block in ((wfc1_hbm, wfc1_s, fc1_block), (wfc2_hbm, wfc2_s, fc2_block)):
        w_parts.append(spread_weight(s, d, block))

    def result(src, dst, k):
        lo, hi = pn.out_cuts[k], pn.out_cuts[k + 1]
        there = dst.at[me, :, pl.ds(lo, hi - lo)]

        def part(m):
            return src.at[pl.ds(aligned(m * CS, CS), CS), pl.ds(lo, hi - lo)]

        return [local_copy(part(me), there)] + [remote(part(peer(d)), there, {"mp": peer(d)}) for d in range(1, n_mp)]

    o_parts = [result(ow_s, orecv_s, k) for k in range(pn.pairs)]
    i_parts = [result(iw_s, irecv_s, k) for k in range(pn.pairs)]

    def rows_of(j, y, rows):
        return pl.ds(aligned(j * rows + y * (rows // 2), 8), rows // 2)

    def fc2_blocks(j, y):
        return [dfc2_ref[rows_of(j, y, pn.FFS), :]]

    def fc1_blocks(j, y):
        at = rows_of(j, y, CS)
        return [dfc1_ref[at, i * C:(i + 1) * C] for i in range(FF // C)] + [dproj_ref[at, :]]

    def third(i):
        return lambda j, y: [dqkv_ref[pl.ds(aligned(j * CS, 8), CS), i * C:(i + 1) * C]]

    blocks = (fc2_blocks, fc1_blocks, third(2), third(1), third(0))
    groups = [Group(pn, g[0], r, f) for g, r, f in zip(pn.groups, group_refs, blocks)]
    for g in groups:
        g.build(remote, local_copy, xi, core, sibling, dp)
    g_fc2, g_fc1, g_v, g_k, g_q = groups
    hop1 = [remote(pack_s.at[peer(d)], hop1_s.at[me], {"mp": peer(d)}) for d in range(1, n_mp)]
    hop2 = [remote(pack2_s, hop2_s.at[dp], {"dp": (dp + e) % n_dp}) for e in range(1, n_dp)]

    def start(copies):
        for c in copies:
            c.start()

    def arrive(copies):
        copies[0].wait()
        for c in copies[1:]:
            c.wait_recv()

    def start_weight(w):
        start(w[1])
        w[0].start()
        w[2].start()

    def spread_along(w):
        if len(w) > 4:
            for a in w[1]:
                a.wait_recv()
            start(w[4])

    def relay_weight(w):
        for a in w[4] if len(w) > 4 else w[1]:
            a.wait_recv()
        start(w[3])

    def have_weight(w):
        own, _, beside, relay = w[:4]
        own.wait()
        beside.wait_recv()
        for r in relay:
            r.wait_recv()

    pvec_ref[...] = jnp.zeros_like(pvec_ref)
    for i, r in enumerate(vec_refs[:-1]):
        pvec_ref[i:i + 1, 0:CS] = r[...].astype(F32)
    long = [vec_refs[-1][i:i + 1, :].astype(F32) for i in range(vec_refs[-1].shape[0])]
    long = jnp.concatenate(long, axis=1)
    for i in range(pn.FFS // CS):
        pvec_ref[len(VECS) + i:len(VECS) + i + 1, 0:CS] = long[:, i * CS:(i + 1) * CS]

    barrier = pltpu.get_barrier_semaphore()
    for d in range(1, n_mp):
        pl.semaphore_signal(barrier, inc=1, device_id={"mp": peer(d)}, device_id_type=MESH)
    for e in range(1, n_dp):
        pl.semaphore_signal(barrier, inc=1, device_id={"dp": (dp + e) % n_dp}, device_id_type=MESH)
    pl.semaphore_wait(barrier, n_mp - 1 + n_dp - 1)

    start(vec_parts)
    start_weight(w_parts[0])
    start(x_parts[0])

    hd = C // HEADS
    factor = hd ** (-0.5)
    head_of = lax.broadcasted_iota(jnp.int32, (1, C), 1) // hd
    for h in range(HEADS):
        pre = post = jnp.zeros((1, C), F32)
        for g in range(HEADS):
            pre = jnp.where(head_of == g, pre_ref[h, g] * factor, pre)
            post = jnp.where(head_of == g, post_ref[g, h], post)
        mrow_s[h:h + 1, :] = pre
        mrow_s[HEADS + h:HEADS + h + 1, :] = post
    mask_s[...] = jnp.full_like(mask_s, MASKED)
    for i in range(n_img):
        keep = keep_ref[pl.ds(me * n_img + i, 1), :]
        mask_s[i:i + 1, 0:PATCHES] = jnp.where(keep > 0, 0.0, MASKED)
    for r in (dqkv_ref, dproj_ref, dfc1_ref, dfc2_ref, dvec_ref, dmix_ref):
        r[...] = jnp.zeros_like(r)

    arrive(vec_parts)
    for m in range(n_mp):
        t = jnp.transpose(jnp.concatenate([pv_s[m], jnp.zeros((TILE - 16, TILE), F32)], axis=0))
        for i in range(pn.vrows):
            if i < len(VECS):
                at = pn.off[VECS[i]][0] + m * CS
            else:
                at = pn.off["fb1"][0] + m * pn.FFS + (i - len(VECS)) * CS
            col_s[at:at + CS, :] = jnp.broadcast_to(t[:CS, i:i + 1], (CS, TILE)).astype(BF16)

    def turn(src, dst):
        rows, cols = src.shape
        for r in range(0, rows, 384):
            for c in range(0, cols, 384):
                dst[c:c + 384, r:r + 384] = jnp.transpose(src[r:r + 384, c:c + 384])

    relay_weight(w_parts[0])
    start(x_parts[1])
    have_weight(w_parts[0])
    turn(wqkv_s, wqkvT_s)

    def col(name, lo=0, hi=None, width=2 * LANES):
        o, w = pn.off[name]
        hi = w if hi is None else hi
        v = twice(col_s[o + lo:o + hi, :].astype(F32))
        return v if width == LANES else twice(v)

    def lanes_of(b):
        return pl.ds(pl.multiple_of(b * LANES, LANES), LANES)

    def lanes_of_pair(k):
        return pl.ds(pl.multiple_of(k * 2 * LANES, 2 * LANES), 2 * LANES)

    def both(f, k):
        return jnp.concatenate([f(2 * k), f(2 * k + 1)], axis=1)

    lane = lax.broadcasted_iota(jnp.int32, (C, TILE), 1)

    def take(src, b):
        s = b * PATCHES + my_shift
        r = s % TILE
        t = s // TILE
        left = (TILE - r) % TILE
        last = (s + PATCHES - 1) // TILE
        parts = [pltpu.roll(src[:, pl.ds(aligned(i * TILE, TILE), TILE)].astype(F32), left, 1)
                 for i in (t, t + 1, last)]
        lo = jnp.where(lane < TILE - r, parts[0], parts[1])
        hi = jnp.where(lane < TILE - r, parts[1], parts[2])
        hi = jnp.where(lane < PATCHES - TILE, hi, 0.0)
        return jnp.concatenate([lo, hi], axis=1)

    def put(dst, b, v):
        s = b * PATCHES + my_shift
        r = s % TILE
        t = s // TILE
        at = [pl.ds(aligned((t + i) * TILE, TILE), TILE) for i in range(3)]
        lo = pltpu.roll(v[:, :TILE], r, 1)
        hi = pltpu.roll(v[:, TILE:], r, 1)
        old = dst[:, at[0]].astype(F32)
        dst[:, at[0]] = jnp.where(lane < r, old, lo).astype(BF16)
        dst[:, at[1]] = jnp.where(lane < r, lo, hi).astype(BF16)
        dst[:, at[2]] = hi.astype(BF16)

    def norm(x):
        mean = jnp.sum(x, axis=0, keepdims=True) * inv_c
        d = x - mean
        inv = lax.rsqrt(jnp.sum(d * d, axis=0, keepdims=True) * inv_c + EPSILON)
        return d * inv, inv

    def norm_back(u, n, inv, g):
        s = u * g
        m1 = jnp.sum(s, axis=0, keepdims=True) * inv_c
        m2 = jnp.sum(s * n, axis=0, keepdims=True) * inv_c
        return inv * (s - m1 - n * m2)

    def add_vec(name, v, lo=0):
        o = pn.off[name][0] + lo
        dvec_ref[o:o + v.shape[0], :] += fold(v)

    def when_each(k, do):
        for j in range(pn.pairs):
            pl.when(k == j)(functools.partial(do, j))

    def steps(k, plan):
        for at, do in plan:
            pl.when(k == at * pn.pairs // 4)(do)

    def start_weights():
        for w in w_parts[1:]:
            start_weight(w)

    def along_weights():
        for w in w_parts[2:]:
            spread_along(w)

    def relay_weights():
        for w in w_parts[1:]:
            relay_weight(w)

    mixed = gh_s.at[0:HEADS * KEYS, 0:C]

    def phase_a(k, _):
        when_each(k, lambda j: arrive(x_parts[j]))
        pl.when(k == 0)(start_weights)
        pl.when(k == min(2, pn.pairs - 1))(along_weights)
        for j in range(2, pn.pairs):
            pl.when(k == j - 1)(functools.partial(start, x_parts[j]))
        for j in range(pn.pairs // 2):
            pl.when(k == j + pn.pairs // 2)(functools.partial(start, c_parts[j]))
        for b in (2 * k, 2 * k + 1):
            at = lanes_of(b)
            x = take(xw_s, b)
            x_s[:, at] = x.astype(BF16)
            n1, _inv = norm(x)
            first = (n1 * col("g1", width=LANES) + col("b1", width=LANES)).astype(BF16)
            first_s[:, at] = first
            q = (dot(wqkvT_s[0:C, :], first) + col("qb", width=LANES)).astype(BF16)
            qkv_s[0:C, at] = q
            kT = dot(wqkvT_s[C:2 * C, :], first).astype(BF16)
            qkv_s[C:2 * C, at] = kT
            vT = (dot(wqkvT_s[2 * C:3 * C, :], first) + col("vb", width=LANES)).astype(BF16)
            qkv_s[2 * C:3 * C, at] = vT
            maskc = twice(lane_column(mask_s[pl.ds(b, 1), :])[:KEYS])
            kr = jnp.transpose(kT.astype(F32))[:KEYS]
            vr = jnp.transpose(vT.astype(F32))[:KEYS]
            for h in range(HEADS):
                rows = slice(h * KEYS, (h + 1) * KEYS)
                kmix = (kr * mrow_s[h:h + 1, :]).astype(BF16)
                logit = dot(kmix, q) + maskc
                top = jnp.max(logit, axis=0, keepdims=True)
                e = jnp.exp(logit - top)
                inv = 1.0 / jnp.sum(e, axis=0, keepdims=True)
                p_s[b, rows, :] = (e * inv).astype(BF16)
                mixed[rows, :] = (vr * mrow_s[HEADS + h:HEADS + h + 1, :]).astype(BF16)
            a_s[:, at] = dot_tn(mixed[...], p_s[b]).astype(BF16)
        return 0

    lax.fori_loop(0, pn.pairs, phase_a, 0)

    relay_weights()
    for w, s, d in zip(w_parts[1:], (wproj_s, wfc1_s, wfc2_s), (wprojT_s, wfc1T_s, wfc2T_s)):
        have_weight(w)
        turn(s, d)

    def phase_b(k, _):
        when_each(k, lambda j: arrive(c_parts[j]))
        for j in range(pn.pairs // 2, pn.pairs):
            pl.when(k == j - pn.pairs // 2)(functools.partial(start, c_parts[j]))
        at = lanes_of_pair(k)
        x = x_s[:, at].astype(F32)
        att = a_s[:, at]
        branch = dot(wprojT_s[...], att) + col("pb")
        middle = x + col("s1") * branch
        n2, inv2 = norm(middle)
        second = (n2 * col("g2") + col("b2")).astype(BF16)
        step = 256
        for r in range(0, FF, step):
            hid = dot(wfc1T_s[r:r + step, :], second) + col("fb1", r, r + step)
            cum, slope = gelu_parts(hid)
            act_s[r:r + step, :] = (hid * cum).astype(BF16)
            slope_s[r:r + step, :] = slope
        mlp = dot(wfc2T_s[...], act_s[0:FF, :]) + col("fb2")
        cot = both(lambda b: take(cw_s, b), k)
        result = middle + col("s2") * mlp
        put(ow_s, 2 * k, result[:, :LANES])
        put(ow_s, 2 * k + 1, result[:, LANES:])
        when_each(k, lambda j: start(o_parts[j]))
        add_vec("s2", cot * mlp)
        g_mlp = (col("s2") * cot).astype(BF16)
        add_vec("fb2", g_mlp.astype(F32))
        for r in range(0, FF, step):
            g_act = dot(wfc2_s[r:r + step, :], g_mlp)
            gh = (g_act * slope_s[r:r + step, :]).astype(BF16)
            gh_s[r:r + step, :] = gh
            add_vec("fb1", gh.astype(F32), r)
            dfc2_ref[r:r + step, :] += dot_nt(act_s[r:r + step, :], g_mlp)
        gh = gh_s[0:FF, :]
        dfc1_ref[...] += dot_nt(second, gh)
        g_second = dot(wfc1_s[...], gh)
        add_vec("g2", g_second * n2)
        add_vec("b2", g_second)
        g_mid = cot + norm_back(g_second, n2, inv2, col("g2"))
        gm_s[:, at] = g_mid
        add_vec("s1", g_mid * branch)
        g_br = (col("s1") * g_mid).astype(BF16)
        add_vec("pb", g_br.astype(F32))
        dproj_ref[...] += dot_nt(att, g_br)
        a_s[:, at] = dot(wproj_s[...], g_br).astype(BF16)
        return 0

    lax.fori_loop(0, pn.pairs, phase_b, 0)

    gt_s = act_s.at[0:HEADS * KEYS, 0:LANES]
    one_s = slope_s.at[0:HEADS * KEYS, 0:C]
    block = 16

    def unmix(wide, rows, side, out):
        parts = []
        for j in range(0, KEYS, block):
            total = jnp.zeros((block, C), F32)
            vj = side[j:j + block]
            for h in range(HEADS):
                wj = wide[h * KEYS + j:h * KEYS + j + block, :]
                total = total + mrow_s[rows + h:rows + h + 1, :] * wj
                t = wj * vj
                dmix_ref[rows + h] += t[:8] + t[8:]
            parts.append(total)
        parts.append(jnp.zeros((LANES - KEYS, C), F32))
        return jnp.transpose(jnp.concatenate(parts, axis=0)).astype(BF16)

    def phase_d(k, _):
        at = lanes_of_pair(k)
        g_first = dot(wqkv_s[...], qkv_s[:, at])
        n1, inv1 = norm(x_s[:, at].astype(F32))
        add_vec("g1", g_first * n1)
        add_vec("b1", g_first)
        grad = gm_s[:, at] + norm_back(g_first, n1, inv1, col("g1"))
        put(iw_s, 2 * k, grad[:, :LANES])
        put(iw_s, 2 * k + 1, grad[:, LANES:])
        when_each(k, lambda j: start(i_parts[j]))
        return 0

    def behind(k):
        phase_d(k, 0)

    def phase_c(k, _):
        for b in (2 * k, 2 * k + 1):
            at = lanes_of(b)
            da = a_s[:, at]
            q = qkv_s[0:C, at]
            kr = jnp.transpose(qkv_s[C:2 * C, at].astype(F32))[:KEYS]
            vr = jnp.transpose(qkv_s[2 * C:3 * C, at].astype(F32))[:KEYS]
            for h in range(HEADS):
                rows = slice(h * KEYS, (h + 1) * KEYS)
                vmix = (vr * mrow_s[HEADS + h:HEADS + h + 1, :]).astype(BF16)
                gs = dot(vmix, da)
                p = p_s[b, rows, :].astype(F32)
                d = jnp.sum(gs * p, axis=0, keepdims=True)
                gt_s[rows, :] = (p * (gs - d)).astype(BF16)
                mixed[rows, :] = (kr * mrow_s[h:h + 1, :]).astype(BF16)
            gq = dot_tn(mixed[...], gt_s[...]).astype(BF16)
            one_s[...] = dot_nt(p_s[b], da)
            two_s[...] = dot_nt(gt_s[...], q)
            gv = unmix(one_s, HEADS, vr, None)
            gk = unmix(two_s, 0, kr, None)
            add_vec("qb", gq.astype(F32))
            add_vec("vb", gv.astype(F32))
            qkv_s[0:C, at] = gq
            qkv_s[C:2 * C, at] = gk
            qkv_s[2 * C:3 * C, at] = gv
        at = lanes_of_pair(k)
        dqkv_ref[...] += dot_nt(first_s[:, at], qkv_s[:, at])
        steps(k, ((0, g_fc2.over_x), (1, g_fc2.over_z), (2, g_fc2.back_z), (2, g_fc1.over_x), (3, g_fc2.back_y),
                  (3, g_fc1.over_z)))
        pl.when(k > 0)(lambda: behind(k - 1))
        return 0

    lent = [c for w in w_parts[1:] for c in w[3] + (w[4] if len(w) > 4 else [])]
    for c in lent:
        c.wait_send()
    g_fc2.over_cores()
    g_fc1.over_cores()
    g_fc2.over_y()
    g_fc1.over_y()
    lax.fori_loop(0, pn.pairs, phase_c, 0)
    for g in (g_v, g_k, g_q):
        g.over_cores()
    lax.fori_loop(pn.pairs - 1, pn.pairs, phase_d, 0)
    for g in (g_v, g_k, g_q):
        g.over_x()

    for m in range(n_mp):
        for i in range(pn.vrows):
            if i < len(VECS):
                o = pn.off[VECS[i]][0] + m * CS
            else:
                o = pn.off["fb1"][0] + m * pn.FFS + (i - len(VECS)) * CS
            block = jnp.concatenate([dvec_ref[o:o + CS, :], jnp.zeros((TILE - CS, TILE), F32)], axis=0)
            pack_s[m, i:i + 1, :] = jnp.sum(jnp.transpose(block), axis=0, keepdims=True)
        pack_s[m, pn.vrows:16, :] = jnp.zeros((16 - pn.vrows, TILE), F32)
    lane_of = lax.broadcasted_iota(jnp.int32, (2 * HEADS, TILE), 1)
    heads = lax.broadcasted_iota(jnp.int32, (2 * HEADS, C), 1) // hd
    dmix = jnp.sum(dmix_ref[...], axis=1)
    mix = jnp.zeros((2 * HEADS, TILE), F32)
    for g in range(HEADS):
        mix = jnp.where(lane_of == g, jnp.sum(jnp.where(heads == g, dmix, 0.0), axis=1, keepdims=True), mix)
    for m in range(n_mp):
        pack_s[m, 16:32, :] = mix
    start(hop1)
    g_fc1.back_z()
    for g in (g_v, g_k, g_q):
        g.over_z()
    hop1_s[me] = pack_s[me]
    for c in hop1:
        c.wait_recv()
    both_hops = hop1_s[0]
    for m in range(1, n_mp):
        both_hops = both_hops + hop1_s[m]
    pack2_s[...] = both_hops
    start(hop2)
    g_fc1.back_y()
    for g in (g_v, g_k, g_q):
        g.back_z()
    hop2_s[dp] = both_hops
    for c in hop2:
        c.wait_recv()
    both_hops = hop2_s[0]
    for e in range(1, n_dp):
        both_hops = both_hops + hop2_s[e]
    small_ref[...] = both_hops
    for g in (g_v, g_k, g_q):
        g.back_y()

    for k in range(pn.pairs):
        arrive(o_parts[k])
        arrive(i_parts[k])
    for g in groups:
        g.finish()
    lent = [id(c) for c in lent]
    for c in sent:
        if id(c) not in lent:
            c.wait_send()


def layer_call(pn, x, cot, ws, keep, pre, post, vecs):
    C, CS, FF, n_img, n_mp, n_dp = pn.C, pn.CS, pn.FF, pn.n_img, pn.n_mp, pn.n_dp
    S = jax.ShapeDtypeStruct
    T = n_img * LANES
    outs = (S((n_mp, CS, pn.width), BF16), S((n_mp, CS, pn.width), BF16), S((32, TILE), F32))
    outs += tuple(S((ny * half, C), BF16) for ny, half, _ in pn.groups)
    V = pltpu.VMEM
    remotes = (4 * pn.pairs + 2) * (n_mp - 1) + 4 * (2 * (pn.nx - 1) + 1)
    remotes += 2 * (3 * pn.nx - 1 + 2 * (n_dp // 2 - 1) + 1) + 3 * (2 * pn.nx - 1 + 2 * (n_dp - 1)) + n_dp - 1
    remotes += 2 * (pn.nx - 1) * 3
    locals_ = 4 * pn.pairs + 1 + 4 + 5
    tall = max(FF, HEADS * KEYS)
    scratch = [V((C, pn.wide), BF16), V((C, pn.wide), BF16), V((n_mp, 16, TILE), F32),
               V((C, 3 * C), BF16), V((C, C), BF16), V((C, FF), BF16), V((FF, C), BF16),
               V((3 * C, C), BF16), V((C, C), BF16), V((FF, C), BF16), V((C, FF), BF16),
               V((C, T), BF16), V((C, T), BF16), V((3 * C, T), BF16), V((n_img, HEADS * KEYS, LANES), BF16),
               V((C, T), BF16), V((C, T), F32), V((pn.total, TILE), BF16), V((tall, 2 * LANES), BF16),
               V((tall, 2 * LANES), F32), V((tall, 2 * LANES), BF16), V((HEADS * KEYS, C), F32),
               V((2 * HEADS, C), F32), V((max(n_img, 8), LANES), F32),
               V((C, 3 * C), F32), V((C, C), F32), V((C, FF), F32), V((FF, C), F32), V((pn.total, TILE), F32),
               V((2 * HEADS, 8, C), F32),
               V((n_mp, 32, TILE), F32), V((n_mp, 32, TILE), F32), V((32, TILE), F32), V((n_dp, 32, TILE), F32),
               V((16, TILE), F32)]
    for g in pn.groups:
        scratch += pn.group_scratch(*g)
    scratch += [pltpu.SemaphoreType.DMA((remotes,)), pltpu.SemaphoreType.DMA((remotes,)),
                pltpu.SemaphoreType.DMA((locals_,))]
    vm = pl.BlockSpec(memory_space=pltpu.VMEM)
    sm = pl.BlockSpec(memory_space=pltpu.SMEM)
    hbm = pl.BlockSpec(memory_space=pl.ANY)
    return pl.pallas_call(
        functools.partial(layer_kernel, pn),
        out_shape=outs,
        in_specs=[hbm] * 6 + [vm] + [sm] * 2 + [vm] * len(vecs),
        out_specs=[hbm, hbm, vm] + [hbm] * len(pn.groups),
        scratch_shapes=scratch,
        compiler_params=pltpu.CompilerParams(vmem_limit_bytes=VMEM_BYTES, collective_id=0, has_side_effects=True),
        name="layer",
    )(x, cot, *ws, keep, pre, post, *vecs)


def finish_kernel(pn, orecv, irecv, small, r_fc2, r_fc1, r_v, r_k, r_q, out_hbm, ig_hbm, gqkv_hbm, gproj_hbm, gfc1_hbm,
                  gfc2_hbm, pre_ref, post_ref, fb1_ref, *rest):
    C, CS, FF = pn.C, pn.CS, pn.FF
    vec_refs, rest = rest[:len(VECS)], rest[len(VECS):]
    o_s, i_s, fc2_s, fc1_s, v_s, k_s, q_s, out_s, ig_s, gqkv_s, gproj_s, gfc1_s, gfc2_s, long_s, sem = rest
    ins = [pltpu.make_async_copy(a, b, sem.at[i]) for i, (a, b) in enumerate(
        ((orecv, o_s), (irecv, i_s), (r_fc2, fc2_s), (r_fc1, fc1_s), (r_v, v_s), (r_k, k_s), (r_q, q_s)))]
    outs = [pltpu.make_async_copy(a, b, sem.at[7 + i]) for i, (a, b) in enumerate(
        ((out_s, out_hbm), (ig_s, ig_hbm), (gfc2_s, gfc2_hbm), (gfc1_s, gfc1_hbm), (gproj_s, gproj_hbm),
         (gqkv_s, gqkv_hbm)))]
    for c in ins:
        c.start()
    lane_out = lax.broadcasted_iota(jnp.int32, (CS, TILE), 1)

    def join(recv, dst):
        for j in range(pn.cols // TILE):
            parts = [(m, j - pn.bases[m] // TILE) for m in range(pn.n_mp)
                     if pn.bases[m] <= j * TILE and j * TILE < pn.bases[m] + pn.shifts[m] + pn.tok]
            v = None
            for m, l in parts:
                w = recv[m, :, l * TILE:(l + 1) * TILE]
                v = w if v is None else jnp.where(lane_out < pn.shifts[m], v.astype(F32), w.astype(F32)).astype(BF16)
            dst[:, j * TILE:(j + 1) * TILE] = v

    def unpack(src, dst, at, lanes, rows):
        for y in range(2):
            lo = y * (src.shape[0] // 2) + at * (rows // 2)
            dst[y * (rows // 2):(y + 1) * (rows // 2), lanes] = src[lo:lo + rows // 2, :].astype(F32)

    pre_ref[...] = small[16:16 + HEADS, 0:HEADS] * (C // HEADS) ** (-0.5)
    pad = jnp.zeros((TILE - HEADS, TILE), F32)
    post_ref[...] = jnp.transpose(jnp.concatenate([small[16 + HEADS:16 + 2 * HEADS, :], pad], axis=0))[0:HEADS, 0:HEADS]
    for i, r in enumerate(vec_refs):
        r[...] = small[i:i + 1, 0:CS]
    for i in range(pn.FFS // CS):
        long_s[0:1, i * CS:(i + 1) * CS] = small[len(VECS) + i:len(VECS) + i + 1, 0:CS]
    rows, lanes = fb1_ref.shape
    for i in range(rows):
        fb1_ref[i:i + 1, :] = long_s[0:1, i * lanes:(i + 1) * lanes]
    ins[0].wait()
    join(o_s, out_s)
    outs[0].start()
    ins[1].wait()
    join(i_s, ig_s)
    outs[1].start()
    ins[2].wait()
    unpack(fc2_s, gfc2_s, 0, slice(0, C), pn.FFS)
    outs[2].start()
    ins[3].wait()
    for i in range(FF // C):
        unpack(fc1_s, gfc1_s, i, slice(i * C, (i + 1) * C), CS)
    outs[3].start()
    unpack(fc1_s, gproj_s, FF // C, slice(0, C), CS)
    outs[4].start()
    for c, src, i in zip(ins[4:], (v_s, k_s, q_s), (2, 1, 0)):
        c.wait()
        gqkv_s[:, i * C:(i + 1) * C] = src[0:CS, :].astype(F32)
    outs[5].start()
    for c in outs:
        c.wait()


def finish_call(pn, parts):
    S = jax.ShapeDtypeStruct
    V = pltpu.VMEM
    C, CS = pn.C, pn.CS
    big = ((CS, pn.cols), (CS, pn.cols), (CS, 3 * C), (CS, C), (CS, pn.FF), (pn.FFS, C))
    outs = tuple(S(b, BF16 if i < 2 else F32) for i, b in enumerate(big))
    outs += (S((HEADS, HEADS), F32), S((HEADS, HEADS), F32), S(pn.long, F32))
    outs += (S((1, CS), F32),) * len(VECS)
    vm = pl.BlockSpec(memory_space=pltpu.VMEM)
    hbm = pl.BlockSpec(memory_space=pl.ANY)
    scratch = [V(p.shape, BF16) for i, p in enumerate(parts) if i != 2]
    scratch += [V(b, BF16 if i < 2 else F32) for i, b in enumerate(big)]
    return pl.pallas_call(
        functools.partial(finish_kernel, pn),
        out_shape=outs,
        in_specs=[hbm, hbm, vm] + [hbm] * (len(parts) - 3),
        out_specs=[hbm] * len(big) + [vm] * (len(outs) - len(big)),
        scratch_shapes=scratch + [V((8, pn.FFS), F32), pltpu.SemaphoreType.DMA((13,))],
        compiler_params=pltpu.CompilerParams(vmem_limit_bytes=VMEM_BYTES),
        name="finish",
    )(*parts)


def local(patches, keep_mask, ln1_gain, ln1_bias, w_qkv, q_bias, v_bias, mix_pre, mix_post, w_proj, proj_bias,
          gamma1, ln2_gain, ln2_bias, w_fc1, fc1_bias, w_fc2, fc2_bias, gamma2, cotangent):
    n_mp, n_dp = lax.axis_size("mp"), lax.axis_size("dp")
    pn = Plan(n_dp, n_mp, patches.shape, keep_mask.shape, w_fc2.shape)
    vecs = (ln1_gain, ln1_bias, q_bias, v_bias, proj_bias, gamma1, ln2_gain, ln2_bias, fc2_bias, gamma2, fc1_bias)
    parts = layer_call(pn, patches, cotangent, (w_qkv, w_proj, w_fc1, w_fc2), keep_mask, mix_pre, mix_post,
                       [v.reshape(1, -1) for v in vecs[:-1]] + [vecs[-1].reshape(pn.long)])
    out, ig, gqkv, gproj, gfc1, gfc2, pre_total, post_total, gfb1, *gs = finish_call(pn, parts)
    gfb1 = gfb1.reshape(-1)
    gs = [g.reshape(-1) for g in gs]
    return (out, ig, gs[0], gs[1], gqkv, gs[2], gs[3], pre_total, post_total, gproj, gs[4], gs[5],
            gs[6], gs[7], gfc1, gfb1, gfc2, gs[8], gs[9])


def solution(mesh):
    m, mn = P("mp"), P("mp", None)
    big = P("mp", "dp")
    in_specs = (big, P("dp", None), m, m, mn, m, m, P(), P(), mn, m, m, m, m, mn, m, mn, m, m, big)
    out_specs = (big, big, m, m, mn, m, m, P(), P(), mn, m, m, m, m, mn, m, mn, m, m)
    return jax.shard_map(local, mesh=mesh, in_specs=in_specs, out_specs=out_specs, check_vma=False)
```

profile of v0, /device:TPU:0, one launch (start us, length us, event | category | flops | bytes accessed | tf_op | source)
XLA Modules:
  0.0 138.5 jit_solution(488422408348191950)
XLA Ops:
  0.7 132.8 %layer.1 = (bf16[4,96,1664]{2,1,0:T(8,128)(2,1)}, bf16[4,96,1664]{2,1,0:T(8,128)(2,1)}, f32[32,128]{1,0:T(8,128)}, bf16[384,384]{1,0:T(8,128)(2,1)}, bf16[512,38...) custom-call(bf16[96,6272]{1,0:T(8,128)(2,1)} %x_hbm.1, ...), custom_call_target="tpu_custom_call" | custom-call | tf_op jit(solution)/shard_map/layer/pallas_call | solution.py:778
  133.4 4.9 %finish.1 = (bf16[96,6272]{1,0:T(8,128)(2,1)}, bf16[96,6272]{1,0:T(8,128)(2,1)}, f32[96,1152]{1,0:T(8,128)}, f32[96,384]{1,0:T(8,128)}, f32[96,1536]{1,0:T(8,128...) custom-call(bf16[4,96,1664]{2,1,0:T(8,128)(2,1)} %get-tuple-element., ...), custom_call_target="tpu_custom_call" | custom-call | tf_op jit(solution)/shard_map/finish/pallas_call | solution.py:863
where the time goes:
time: 139 us; the launch traced here: 138 us
  Pallas kernels  138 us (99%)
    pallas_call x1, Pallas kernels, layer_call(): pl.pallas_call(functools.partial(layer_kernel, pn), out_shape=outs, in_sp...  133 us
    pallas_call x1, Pallas kernels, finish_call(): pl.pallas_call(functools.partial(finish_kernel, pn), out_shape=outs, in_s...  4.87 us

commit v1 on v0

--- a/solution.py
+++ b/solution.py
@@ -688,9 +688,9 @@
     lax.fori_loop(0, pn.pairs, phase_c, 0)
     for g in (g_v, g_k, g_q):
         g.over_cores()
-    lax.fori_loop(pn.pairs - 1, pn.pairs, phase_d, 0)
     for g in (g_v, g_k, g_q):
         g.over_x()
+    lax.fori_loop(pn.pairs - 1, pn.pairs, phase_d, 0)
 
     for m in range(n_mp):
         for i in range(pn.vrows):

time: 139 us -> 137 us (0.986)
  Pallas kernels: 138 us -> 136 us
    pallas_call x1, Pallas kernels: 133 us -> 131 us  [layer_call(): pl.pallas_call(functools.partial(layer_kernel, pn), out_shape=outs, in_sp...]
where the time goes in v1:
time: 137 us
  Pallas kernels  136 us (99%)
    pallas_call x1, Pallas kernels, layer_call(): pl.pallas_call(functools.partial(layer_kernel, pn), out_shape=outs, in_sp...  131 us
    pallas_call x1, Pallas kernels, finish_call(): pl.pallas_call(functools.partial(finish_kernel, pn), out_shape=outs, in_s...  4.87 us

profile of v1, /device:TPU:0, one launch (start us, length us, event | category | flops | bytes accessed | tf_op | source)
XLA Modules:
  0.0 136.9 jit_solution(5556826435653833110)
XLA Ops:
  0.7 131.1 %layer.1 = (bf16[4,96,1664]{2,1,0:T(8,128)(2,1)}, bf16[4,96,1664]{2,1,0:T(8,128)(2,1)}, f32[32,128]{1,0:T(8,128)}, bf16[384,384]{1,0:T(8,128)(2,1)}, bf16[512,38...) custom-call(bf16[96,6272]{1,0:T(8,128)(2,1)} %x_hbm.1, ...), custom_call_target="tpu_custom_call" | custom-call | tf_op jit(solution)/shard_map/layer/pallas_call | solution.py:778
  131.8 4.9 %finish.1 = (bf16[96,6272]{1,0:T(8,128)(2,1)}, bf16[96,6272]{1,0:T(8,128)(2,1)}, f32[96,1152]{1,0:T(8,128)}, f32[96,384]{1,0:T(8,128)}, f32[96,1536]{1,0:T(8,128...) custom-call(bf16[4,96,1664]{2,1,0:T(8,128)(2,1)} %get-tuple-element., ...), custom_call_target="tpu_custom_call" | custom-call | tf_op jit(solution)/shard_map/finish/pallas_call | solution.py:863

commit v2 on v1

--- a/solution.py
+++ b/solution.py
@@ -102,8 +102,8 @@
 
 
 class Group:
-    def __init__(self, pn, ny, refs, blocks):
-        self.pn, self.ny, self.blocks = pn, ny, blocks
+    def __init__(self, pn, ny, first, refs, blocks):
+        self.pn, self.ny, self.first_owner, self.blocks = pn, ny, first, blocks
         self.nz = pn.n_dp // ny
         self.s1, self.r1, self.s2, self.r2, self.s3, self.r3, self.s4, self.r4, self.s5, self.out = refs
         self.half = self.s4.shape[0]
@@ -123,16 +123,38 @@
         used = pn.CS if ny == 1 else half
         self.c3 = [remote(self.s3.at[d - 1, pl.ds(0, used), :], self.r3.at[d - 1, pl.ds(0, used), :], {"mp": ((xi + d) % pn.nx) * 2 + core})
                    for d in range(1, pn.nx)]
+        self.real = -(-used // self.piece)
+        self.p = self.piece_of(self.z)
         self.c4, self.c5 = [], []
-        own = self.s5.at[self.rows(self.z)]
+        own = self.s5.at[self.rows(self.p)]
         for e in range(1, self.nz):
             to = (self.z + e) % self.nz
-            self.c4.append(remote(self.s4.at[self.rows(to)], self.r4.at[e], {"dp": ny * to + self.y}))
+            self.c4.append(remote(self.s4.at[self.rows(self.piece_of(to))], self.r4.at[e], {"dp": ny * to + self.y}))
             self.c5.append(remote(own, own, {"dp": ny * to + self.y}))
         there = self.out.at[pl.ds(pl.multiple_of(self.y * half, 16), half), :]
         self.c6 = [local_copy(self.s5, there)]
         if ny > 1:
             self.c6.append(remote(self.s5, there, {"dp": other}))
+
+    def piece_of(self, z):
+        return (z + self.nz - self.first_owner) % self.nz
+
+    def only(self, piece, do):
+        if self.real == self.nz:
+            do()
+        else:
+            pl.when(piece < self.real)(do)
+
+    def scattered(self, wait):
+        for e in range(1, self.nz):
+            self.only(self.piece_of((self.z + e) % self.nz), lambda: wait(self.c4[e - 1]))
+
+    def gathered(self, wait):
+        def each():
+            for c in self.c5:
+                wait(c)
+
+        self.only(self.p, each)
 
     def rows(self, q):
         return pl.ds(pl.multiple_of(q * self.piece, 16), self.piece)
@@ -187,21 +209,23 @@
             return v
 
         self.fill(self.s4, 2 * self.xi + self.core, self.y, add)
-        for c in self.c4:
-            c.start()
+        self.scattered(lambda c: c.start())
 
     def back_z(self):
-        v = self.s4[self.rows(self.z), :].astype(F32)
+        def own():
+            v = self.s4[self.rows(self.p), :].astype(F32)
+            for e in range(1, self.nz):
+                self.c4[e - 1].wait_recv()
+                v = v + self.r4[e].astype(F32)
+            self.s5[self.rows(self.p), :] = v.astype(BF16)
+            for c in self.c5:
+                c.start()
+
+        self.only(self.p, own)
+
+    def back_y(self):
         for e in range(1, self.nz):
-            self.c4[e - 1].wait_recv()
-            v = v + self.r4[e].astype(F32)
-        self.s5[self.rows(self.z), :] = v.astype(BF16)
-        for c in self.c5:
-            c.start()
-
-    def back_y(self):
-        for c in self.c5:
-            c.wait_recv()
+            self.only(self.piece_of((self.z + self.nz - e) % self.nz), lambda: self.c5[e - 1].wait_recv())
         for c in self.c6:
             c.start()
 
@@ -346,7 +370,8 @@
         return lambda j, y: [dqkv_ref[pl.ds(aligned(j * CS, 8), CS), i * C:(i + 1) * C]]
 
     blocks = (fc2_blocks, fc1_blocks, third(2), third(1), third(0))
-    groups = [Group(pn, g[0], r, f) for g, r, f in zip(pn.groups, group_refs, blocks)]
+    firsts = (0, 0, 0, n_dp // 4, n_dp // 2)
+    groups = [Group(pn, g[0], o, r, f) for g, o, r, f in zip(pn.groups, firsts, group_refs, blocks)]
     for g in groups:
         g.build(remote, local_copy, xi, core, sibling, dp)
     g_fc2, g_fc1, g_v, g_k, g_q = groups
@@ -740,6 +765,10 @@
     for g in groups:
         g.finish()
     lent = [id(c) for c in lent]
+    lent += [id(c) for g in groups for c in g.c4 + g.c5]
+    for g in groups:
+        g.scattered(lambda c: c.wait_send())
+        g.gathered(lambda c: c.wait_send())
     for c in sent:
         if id(c) not in lent:
             c.wait_send()

time: 137 us -> 136 us (level)
  no operation moved by 1% of the time
where the time goes in v2:
time: 136 us
  Pallas kernels  135 us (99%)
    pallas_call x1, Pallas kernels, layer_call(): pl.pallas_call(functools.partial(layer_kernel, pn), out_shape=outs, in_sp...  130 us
    pallas_call x1, Pallas kernels, finish_call(): pl.pallas_call(functools.partial(finish_kernel, pn), out_shape=outs, in_s...  4.87 us

profile of v2, /device:TPU:0, one launch (start us, length us, event | category | flops | bytes accessed | tf_op | source)
XLA Modules:
  0.0 136.0 jit_solution(6872212853591802171)
XLA Ops:
  0.7 130.3 %layer.1 = (bf16[4,96,1664]{2,1,0:T(8,128)(2,1)}, bf16[4,96,1664]{2,1,0:T(8,128)(2,1)}, f32[32,128]{1,0:T(8,128)}, bf16[384,384]{1,0:T(8,128)(2,1)}, bf16[512,38...) custom-call(bf16[96,6272]{1,0:T(8,128)(2,1)} %x_hbm.1, ...), custom_call_target="tpu_custom_call" | custom-call | tf_op jit(solution)/shard_map/layer/pallas_call | solution.py:807
  131.0 4.9 %finish.1 = (bf16[96,6272]{1,0:T(8,128)(2,1)}, bf16[96,6272]{1,0:T(8,128)(2,1)}, f32[96,1152]{1,0:T(8,128)}, f32[96,384]{1,0:T(8,128)}, f32[96,1536]{1,0:T(8,128...) custom-call(bf16[4,96,1664]{2,1,0:T(8,128)(2,1)} %get-tuple-element., ...), custom_call_target="tpu_custom_call" | custom-call | tf_op jit(solution)/shard_map/finish/pallas_call | solution.py:892
